TPU v7x, 32 devices: a whole 2x2x4 slice. The times are simulated.
32 devices in a mesh: seq: 4 (over x, core), head: 4 (over z), batch: 2 (over y).
Axes of the slice: x: 2, y: 2, z: 4, core: 2. Of those that a mesh axis runs over, the one named last changes fastest.
Arguments:
- hyena_inputs: bfloat16 [4096, 3, 8192], P(('batch', 'seq'), None, 'head'), parts along dimension 0, may hold values from -6 to 6
- short_filter: float32 [3, 3, 8192], P(None, None, 'head'), may hold values from -3.5 to 3.5
- medium_filter: float32 [128, 8192], P(None, 'head'), may hold values from -0.5 to 0.5
- q_proj: bfloat16 [4096, 8192], P(('batch', 'seq'), 'head'), parts along dimension 0, may hold values from -8 to 8
- k_proj: bfloat16 [4096, 8192], P(('batch', 'seq'), 'head'), parts along dimension 0, may hold values from -8 to 8
- out_weight: bfloat16 [8192, 8192], P('head'), may hold values from -0.25 to 0.25
Outputs:
- hyena_out: bfloat16 [4096, 8192], P(('batch', 'seq'), 'head'), parts along dimension 0
- mixed: bfloat16 [4096, 8192], P(('batch', 'seq'), 'head'), parts along dimension 0
There are 2 independent parts, one for each index of `batch`. A program takes and returns all parts, laid end to end along the dimension named above; an argument that names none is the same for every part. Nothing has to cross between parts.
All inputs are finite; a program needn't handle non-finite values.
Results may differ from a plain program's by a relative error of at most 0.011.
Values may be sent and summed in bfloat16 or wider, within the bound.
A program may use at most 192 MiB of HBM per device.

v0:
```python
import math
import jax
import jax.numpy as jnp
from jax import lax
from jax.sharding import PartitionSpec as P

HEAD_SIZE = 128


def passed_along(x, axis, by):
    length = lax.axis_size(axis)
    pairs = [(i, i + by) for i in range(length) if 0 <= i + by < length]
    return lax.ppermute(x, axis, pairs)


def causal_depthwise(extended, taps, out_rows):
    tap_count = taps.shape[0]
    window = extended[extended.shape[0] - out_rows - tap_count + 1 :]
    kernel = taps[::-1][:, None, :]
    result = lax.conv_general_dilated(
        window[None],
        kernel,
        (1,),
        "VALID",
        feature_group_count=extended.shape[1],
        dimension_numbers=("NWC", "WIO", "NWC"),
        precision=lax.Precision.HIGHEST,
    )
    return result[0]


def per_device(hyena_inputs, short_filter, medium_filter, q_proj, k_proj, out_weight):
    tok_rows = hyena_inputs.shape[0]
    chan_width = hyena_inputs.shape[2]
    short_taps = short_filter.shape[1]
    med_taps = medium_filter.shape[0]
    short_table = jnp.transpose(short_filter, (1, 0, 2)).reshape(short_taps, 3 * chan_width)
    input_margin = passed_along(hyena_inputs[tok_rows - (short_taps - 1) :], "seq", 1)
    joined = (
        jnp.concatenate([input_margin, hyena_inputs], 0)
        .astype(jnp.float32)
        .reshape(-1, 3 * chan_width)
    )
    filtered = causal_depthwise(joined, short_table, tok_rows).reshape(tok_rows, 3, chan_width)
    product = (filtered[:, 1] * filtered[:, 2]).astype(jnp.bfloat16)
    product_margin = passed_along(product[tok_rows - (med_taps - 1) :], "seq", 1)
    product_ext = jnp.concatenate([product_margin, product], 0)
    medium = causal_depthwise(product_ext.astype(jnp.float32), medium_filter, tok_rows)
    hyena_out = (filtered[:, 0] * medium).astype(jnp.bfloat16)
    head_count = chan_width // HEAD_SIZE
    score_scale = HEAD_SIZE ** (-0.5)
    seq_index = lax.axis_index("seq")
    queries = q_proj.reshape(tok_rows, head_count, HEAD_SIZE)
    query_pos = seq_index * tok_rows + jnp.arange(tok_rows, dtype=jnp.int32)
    last_query = seq_index * tok_rows + tok_rows - 1
    initial = (
        jnp.zeros((head_count, tok_rows, HEAD_SIZE), jnp.float32),
        jnp.full((head_count, tok_rows), -1e30, jnp.float32),
        jnp.zeros((head_count, tok_rows), jnp.float32),
    )
    carried = initial
    first_row = jnp.int32(0)
    key_piece = lax.all_gather(k_proj, "seq", axis=0, tiled=True)
    value_piece = lax.all_gather(hyena_out, "seq", axis=0, tiled=True)
    piece_rows = key_piece.shape[0]
    block_rows = math.gcd(piece_rows, 512)
    block_count = piece_rows // block_rows
    key_blocks = key_piece.reshape(block_count, block_rows, head_count, HEAD_SIZE)
    value_blocks = value_piece.reshape(block_count, block_rows, head_count, HEAD_SIZE)

    def visit(running, block_item):
        key_blk, value_blk, block_number = block_item
        key_start = first_row + block_number * block_rows

        def attend(current):
            weighted, run_max, total_sum = current
            scores = (
                jnp.einsum("qhd,khd->hqk", queries, key_blk, preferred_element_type=jnp.float32)
                * score_scale
            )
            key_pos = key_start + jnp.arange(block_rows, dtype=jnp.int32)
            allowed = key_pos[None, None, :] <= query_pos[None, :, None]
            masked = jnp.where(allowed, scores, -jnp.inf)
            new_max = jnp.maximum(run_max, jnp.max(masked, axis=-1))
            weights = jnp.exp(masked - new_max[..., None])
            factor = jnp.exp(run_max - new_max)
            new_total = total_sum * factor + jnp.sum(weights, axis=-1)
            new_weighted = weighted * factor[..., None] + jnp.einsum(
                "hqk,khd->hqd",
                weights.astype(jnp.bfloat16),
                value_blk,
                preferred_element_type=jnp.float32,
            )
            return (new_weighted, new_max, new_total)

        def keep_state(current):
            return current

        return (lax.cond(key_start <= last_query, attend, keep_state, running), None)

    carried, unused = lax.scan(
        visit, carried, (key_blocks, value_blocks, jnp.arange(block_count, dtype=jnp.int32))
    )
    weighted, run_max, total_sum = carried
    attended = (
        (weighted / total_sum[..., None])
        .transpose(1, 0, 2)
        .reshape(tok_rows, chan_width)
        .astype(jnp.bfloat16)
    )
    summed = lax.psum_scatter(
        lax.dot_general(
            out_weight, attended, (((0,), (1,)), ((), ())), preferred_element_type=jnp.float32
        ).astype(jnp.bfloat16),
        "head",
        scatter_dimension=0,
        tiled=True,
    ).astype(jnp.float32)
    return (hyena_out, summed.T.astype(jnp.bfloat16))


def solution(mesh):
    return jax.shard_map(
        per_device,
        mesh=mesh,
        in_specs=(
            P(("batch", "seq"), None, "head"),
            P(None, None, "head"),
            P(None, "head"),
            P(("batch", "seq"), "head"),
            P(("batch", "seq"), "head"),
            P("head", None),
        ),
        out_specs=(P(("batch", "seq"), "head"), P(("batch", "seq"), "head")),
        check_vma=False,
    )
```

profile of v0, /device:TPU:0, one launch (start us, length us, event | category | flops | bytes accessed | tf_op | source)
XLA Modules:
  0.0 636.0 jit_solution(6922452532543686896)
XLA Ops:
  10.6 16.9 %rev.6 = f32[3,6144]{1,0:T(4,128)S(1)} reverse(f32[3,6144]{1,0:T(4,128)} %bitcast.76), dimensions={0} | reverse | bytes 147456 | tf_op jit(solution)/shard_map/rev | solution.py:19
  27.6 7.8 %pad_maximum_fusion = bf16[514,3,2048]{2,0,1:T(8,128)(2,1)} fusion(bf16[512,3,2048]{2,0,1:T(8,128)(2,1)} %param.10, bf16[2,3,2048]{2,0,1:T(2,128)(2,1)S(1)} %collective-permute-done), kind=kLoop, calls=%fused_computation.37 | loop fusion | flops 12632064 | bytes 12632064 | tf_op jit(solution)/shard_map/concatenate | solution.py:40
  35.4 9.7 %copy.12 = bf16[514,3,2048]{0,2,1:T(8,128)(2,1)} copy(bf16[514,3,2048]{2,0,1:T(8,128)(2,1)} %pad_maximum_fusion) | data formatting | bytes 12632064 | tf_op jit(solution)/shard_map/concatenate | solution.py:40
  45.1 7.0 %pad = bf16[1,520,6144]{1,2,0:T(8,128)(2,1)} pad(bf16[1,514,6144]{1,2,0:T(8,128)(2,1)} %bitcast.69, bf16[]{:T(256)} %constant.51), padding=0_0x0_6x0_0 | pad | bytes 12705794 | tf_op jit(solution)/shard_map/broadcast_in_dim;reshape | solution.py:21
  52.1 20.5 %reshape.76 = bf16[1,8,65,6144]{2,1,3,0:T(8,128)(2,1)} reshape(bf16[1,520,6144]{1,2,0:T(8,128)(2,1)} %pad) | data formatting | bytes 12779520 | tf_op jit(solution)/shard_map/conv_general_dilated | solution.py:20
  72.7 16.8 %copy.15 = bf16[1,8,65,6144]{3,1,2,0:T(8,128)(2,1)} copy(bf16[1,8,65,6144]{2,1,3,0:T(8,128)(2,1)} %reshape.76) | data formatting | bytes 12779520 | tf_op jit(solution)/shard_map/conv_general_dilated | solution.py:20
  90.4 11.8 %fusion.30 = f32[8,65,6144]{2,0,1:T(8,128)} fusion(f32[3,1,6144]{2,1,0:T(1,128)S(1)} %broadcast_in_dim.40, bf16[1,7,2,6144]{3,1,2,0:T(8,128)(2,1)S(1)} %slice.26, bf16[1,8,65,6144]{3,1,2,0:T(8,128)(2,1)} %copy.15, pred[8,65]{0,1:T(8,128)(4,1)S(1)} %copy-done.4), kind=kOutput, calls=%fused_computation.33 | convolution fusion | flops 137969664 | bytes 19415560 | tf_op jit(solution)/shard_map/conv_general_dilated | solution.py:20
  102.2 17.2 %copy.16 = f32[8,65,6144]{2,1,0:T(8,128)} copy(f32[8,65,6144]{2,0,1:T(8,128)} %fusion.30) | data formatting | bytes 25559040 | tf_op jit(solution)/shard_map/conv_general_dilated | solution.py:20
  119.4 11.3 %reshape.72 = f32[1,520,6144]{2,1,0:T(8,128)} reshape(f32[8,65,6144]{2,1,0:T(8,128)} %copy.16) | data formatting | bytes 25559040 | tf_op jit(solution)/shard_map/conv_general_dilated | solution.py:20
  130.7 10.6 %slice.27 = f32[1,512,6144]{2,1,0:T(8,128)} slice(f32[1,520,6144]{2,1,0:T(8,128)} %reshape.72), slice={[0:1], [0:512], [0:6144]} | slice | bytes 25165824 | tf_op jit(solution)/shard_map/conv_general_dilated | solution.py:20
  141.3 12.8 %copy.17 = f32[1,512,6144]{1,2,0:T(8,128)} copy(f32[1,512,6144]{2,1,0:T(8,128)} %slice.27) | data formatting | bytes 25165824 | tf_op jit(solution)/shard_map/conv_general_dilated | solution.py:20
  154.0 7.7 %fusion.44 = (f32[512,1,2048]{0,2,1:T(8,128)}, bf16[512,1,2048]{0,2,1:T(8,128)(2,1)S(1)}) fusion(f32[512,3,2048]{0,2,1:T(8,128)} %bitcast.66), kind=kLoop, calls=%fused_computation.51 | loop fusion | flops 2097152 | bytes 18874368 | tf_op jit(solution)/shard_map/slice | solution.py:49
  162.8 5.4 collective-permute-start.1
  168.2 5.2 rev.7
  173.3 5.5 copy.33
  178.8 4.0 maximum_bitcast_fusion
  182.8 11.5 %copy.20 = bf16[1,639,2048]{2,0,1:T(2,128)(2,1)} copy(bf16[1,639,2048]{1,2,0:T(8,128)(2,1)} %maximum_bitcast_fusion) | data formatting | bytes 5234688 | tf_op jit(solution)/shard_map/broadcast_in_dim | solution.py:21
  194.4 48.5 %fusion.39 = f32[1,512,2048]{2,0,1:T(1,128)S(1)} fusion(bf16[1,639,2048]{2,0,1:T(2,128)(2,1)} %copy.20, f32[128,1,2048]{2,0,1:T(8,128)S(1)} %bitcast.75), kind=kOutput, calls=%fused_computation.45 | convolution fusion | flops 1610612736 | bytes 7860224 | tf_op jit(solution)/shard_map/conv_general_dilated | solution.py:20
  248.4 3.0 copy.24
  251.5 10.9 %copy.34 = bf16[256,8,16,128]{3,2,1,0:T(8,128)(2,1)} copy(bf16[256,8,16,128]{3,1,2,0:T(8,128)(2,1)} %bitcast.71) | data formatting | bytes 16777216
  262.3 8.8 %copy.23 = bf16[4,512,16,128]{3,1,2,0:T(8,128)(2,1)} copy(bf16[4,512,16,128]{3,2,1,0:T(8,128)(2,1)} %bitcast.67) | data formatting | bytes 16777216
  271.2 33.2 %all-gather.5.cloned.1.call-done = bf16[2048,2048]{1,0:T(8,128)(2,1)} async-done(((bf16[512,2048]{1,0:T(8,128)(2,1)}), bf16[2048,2048]{1,0:T(8,128)(2,1)}) %all-gather.5.cloned.1.call-update) | async-done | bytes 8388624 | tf_op jit(solution)/shard_map/all_gather | solution.py:64
  304.4 9.8 %copy.35 = bf16[256,8,16,128]{3,2,1,0:T(8,128)(2,1)} copy(bf16[256,8,16,128]{3,1,2,0:T(8,128)(2,1)} %bitcast.72) | data formatting | bytes 16777216
  314.1 8.8 %copy.25 = bf16[4,512,16,128]{3,1,2,0:T(8,128)(2,1)} copy(bf16[4,512,16,128]{3,2,1,0:T(8,128)(2,1)} %bitcast.68) | data formatting | bytes 16777216
  325.4 35.2 %while.15 = (s32[]{:T(128)}, f32[16,512,128]{2,1,0:T(8,128)}, f32[16,512]{1,0:T(8,128)S(1)}, f32[16,512]{1,0:T(8,128)S(1)}, s32[4]{0:T(128)S(1)}, /*index=5*/s32...) while((s32[]{:T(128)}, f32[16,512,128]{2,1,0:T(8,128)}, ...), condition=%wide.region_5.6_spmd.clone, body=%wide.region_0.5_spmd.clone.sunk | while | flops 2195997696 | bytes 66598184 | solution.py:101
  326.9 30.0 %conditional.3 = ((f32[16,512,128]{2,1,0:T(8,128)}, f32[16,512]{1,0:T(8,128)S(1)}, f32[16,512]{1,0:T(8,128)S(1)})) conditional(s32[]{:T(128)} %convert_element_type.60, (f32[16,512,128]{2,1,0:T(8,128)}, f32[16,512]{1,0:T(8,128)S(1)}, f32[16,512]{1,0:T(8,128)S(1)}) %tuple.46, (s32[]{:T(128)}, s32[]{:T(128)}, bf16[4,512,16,128]{3,1,2,0:T(8,128)(2,1)}, ...), branch_computations={%region_1.1_spmd, %region_2.4_spmd} | conditional | flops 2195997696 | bytes 66595880 | solution.py:99
  327.1 8.8 %fusion.4 = (f32[16,512]{1,0:T(8,128)S(1)}, f32[16,512,512]{2,1,0:T(8,128)}) fusion(pred[512,512]{0,1:T(8,128)(4,1)S(1)} %broadcast_compare_fusion, bf16[512,16,128]{2,0,1:T(8,128)(2,1)S(1)} %get-tuple-element.117, bf16[4,512,16,128]{3,1,2,0:T(8,128)(2,1)} %get-tuple-element.115, s32[]{:T(128)} %get-tuple-element.116), kind=kOutput, calls=%fused_computation.5 | convolution fusion | flops 1086316544 | bytes 21266944 | tf_op jit(solution)/shard_map/while/body/eval_jaxpr/cond/branch_1_fun/qhd,khd->hqk/dot_general | solution.py:78
  335.9 9.1 %fusion.2 = f32[16,512]{1,0:T(8,128)S(1)} fusion(f32[16,512,512]{2,1,0:T(8,128)} %get-tuple-element.212, f32[16,512]{1,0:T(8,128)S(1)} %max.4, pred[512,512]{0,1:T(8,128)(4,1)S(1)} %broadcast_compare_fusion), kind=kLoop, calls=%fused_computation.3 | loop fusion | flops 16769024 | bytes 17104896 | tf_op jit(solution)/shard_map/while/body/eval_jaxpr/cond/branch_1_fun/reduce_sum | solution.py:87
  345.1 11.7 %multiply_add_fusion = f32[16,512,128]{2,1,0:T(8,128)} fusion(f32[16,512,128]{2,1,0:T(8,128)} %get-tuple-element.111, f32[16,512]{1,0:T(8,128)S(1)} %get-tuple-element.210, bf16[4,512,16,128]{3,1,2,0:T(8,128)(2,1)} %get-tuple-element.118, s32[]{:T(128)} %get-tuple-element.116, f32[16,512,512]{2,1,0:T(8,128)} %get-tuple-element.212, f32[16,512]{1,0:T(8,128)S(1)} %max.4, ...), kind=kOutput, calls=%fused_computation.11 | convolution fusion | flops 1092616192 | bytes 27591168 | tf_op jit(solution)/shard_map/while/body/eval_jaxpr/cond/branch_1_fun/hqk,khd->hqd/dot_general | solution.py:88
  360.6 5.4 copy.26
  368.8 26.1 %fusion.25 = bf16[8192,512]{0,1:T(8,128)(2,1)} fusion(bf16[512,2048]{0,1:T(8,128)(2,1)S(1)} %bitcast.74, bf16[2048,8192]{1,0:T(8,128)(2,1)} %param.15), kind=kOutput, calls=%fused_computation.29 | convolution fusion | flops 17184063488 | bytes 44040192 | tf_op jit(solution)/shard_map/dot_general | solution.py:112
  395.0 234.0 %reduce-scatter.2.cloned.1.call-done = bf16[2048,512]{0,1:T(8,128)(2,1)} async-done(((bf16[8192,512]{0,1:T(8,128)(2,1)}), bf16[2048,512]{0,1:T(8,128)(2,1)}) %reduce-scatter.2.cloned.1.call-update) | async-done | bytes 2097168 | tf_op jit(solution)/shard_map/reduce_scatter | solution.py:111
  (47 shorter events, 18.9 us)
Async XLA Ops:
  7.2 244.3 %all-gather.3.cloned.1.call-start = ((), (), s32[]{:S(2)}) async-start(), calls=%async_computation.1 | async-start | bytes 10485760 | tf_op jit(solution)/shard_map/all_gather | solution.py:63
  8.1 19.4 %collective-permute-start = (bf16[2,3,2048]{2,0,1:T(2,128)(2,1)S(1)}, bf16[2,3,2048]{2,0,1:T(2,128)(2,1)S(1)}, u32[]{:S(2)}, u32[]{:S(2)}) collective-permute-start(bf16[2,3,2048]{2,0,1:T(2,128)(2,1)S(1)} %slice.18), channel_id=1, source_target_pairs={{0,8},{8,16},{16,24},{1,9},{9,17},{17,25},{2,10},{10,18},{18,26},{... | collective-permute-start | bytes 73736 | tf_op jit(solution)/shard_map/ppermute | solution.py:13
  10.5 293.8 %all-gather.5.cloned.1.call-start = ((), (), s32[]{:S(2)}) async-start(), calls=%async_computation.2 | async-start | bytes 10485760 | tf_op jit(solution)/shard_map/all_gather | solution.py:64
  72.7 17.8 %copy-start.4 = (pred[8,65]{0,1:T(8,128)(4,1)S(1)}, pred[8,65]{0,1:T(8,128)(4,1)}, u32[]{:S(2)}) copy-start(pred[8,65]{0,1:T(8,128)(4,1)} %constant.55) | copy-start | bytes 1564
  154.0 14.1 %copy-start.2 = (f32[128,2048]{1,0:T(8,128)S(1)}, f32[128,2048]{1,0:T(8,128)}, u32[]{:S(2)}) copy-start(f32[128,2048]{1,0:T(8,128)} %param.12) | copy-start | bytes 3145732
  162.8 16.0 %collective-permute-start.1 = (bf16[127,2048]{0,1:T(8,128)(2,1)}, bf16[127,2048]{0,1:T(8,128)(2,1)}, u32[]{:S(2)}, u32[]{:S(2)}) collective-permute-start(bf16[127,2048]{0,1:T(8,128)(2,1)} %slice_bitcast_fusion), channel_id=1, source_target_pairs={{0,8},{8,16},{16,24},{1,9},{9,17},{17,25},{2,10},{10,18},{18,26},{... | collective-permute-start | bytes 1560584 | tf_op jit(solution)/shard_map/ppermute | solution.py:13
  178.8 15.6 %copy-start.3 = (f32[128,2048]{1,0:T(8,128)S(1)}, f32[128,2048]{1,0:T(8,128)}, u32[]{:S(2)}) copy-start(f32[128,2048]{1,0:T(8,128)} %rev.7) | copy-start | bytes 3145732
  194.4 48.5 %copy-start = (f32[512,1,2048]{2,0,1:T(8,128)S(1)}, f32[512,1,2048]{2,0,1:T(8,128)}, u32[]{:S(2)}) copy-start(f32[512,1,2048]{2,0,1:T(8,128)} %copy.33) | copy-start | bytes 12582916
  242.9 2.8 copy-start.1
  245.6 383.4 %reduce-scatter.2.cloned.1.call-start = ((), (), s32[]{:S(2)}) async-start(), calls=%async_computation.3 | async-start | bytes 10485760 | tf_op jit(solution)/shard_map/reduce_scatter | solution.py:111
Sparse Core Ops, SparseCore 0:
  10.6 60.8 all-gather.2
  245.7 58.5 all-gather.4
  395.1 233.8 reduce-scatter.1
where the time goes:
time: 644 us; the launch traced here: 636 us
  waiting for transfers between devices  267 us (41%)
  local copies, waits for them, and re-layouts  202 us (31%)
  matrix products  107 us (17%)
  other arithmetic  34.5 us (5%)
  between operations  14.4 us (2%)
  starting transfers between devices  7.87 us (1%)
    reduce_scatter x1, waiting for transfers between devices, per_device(): lax.psum_scatter(lax.dot_general(out_weight, attended, (((0,), (1,)), (()...  234 us
    conv_general_dilated x7, local copies, waits for them, and re-layouts, causal_depthwise(): lax.conv_general_dilated(window[None], kernel, (1,), 'VALID', feature_gro...  90.1 us
    conv_general_dilated x2, matrix products, causal_depthwise(): lax.conv_general_dilated(window[None], kernel, (1,), 'VALID', feature_gro...  60.3 us
    unnamed x17, local copies, waits for them, and re-layouts  49.5 us
    all_gather x1, waiting for transfers between devices, per_device(): value_piece = lax.all_gather(hyena_out, 'seq', axis=0, tiled=True)  33.2 us
    dot_general x1, matrix products, per_device(): lax.dot_general(out_weight, attended, (((0,), (1,)), ((), ())), preferred...  26.1 us
    rev x2, local copies, waits for them, and re-layouts, causal_depthwise(): kernel = taps[::-1][:, None, :]  22.1 us
  transfers between devices with their start and end apart: 5, of which 2 were waited for; matrix products, arithmetic and copies ran while one was open for 40% of the time, Pallas kernels for 0%

commit v1 on v0

--- a/solution.py
+++ b/solution.py
@@ -60,8 +60,11 @@
     )
     carried = initial
     first_row = jnp.int32(0)
-    key_piece = lax.all_gather(k_proj, "seq", axis=0, tiled=True)
-    value_piece = lax.all_gather(hyena_out, "seq", axis=0, tiled=True)
+    key_piece, value_piece = jnp.split(
+        lax.all_gather(jnp.concatenate([k_proj, hyena_out], axis=1), "seq", axis=0, tiled=True),
+        [k_proj.shape[1]],
+        axis=1,
+    )
     piece_rows = key_piece.shape[0]
     block_rows = math.gcd(piece_rows, 512)
     block_count = piece_rows // block_rows

time: 644 us -> 725 us (1.13)
  waiting for transfers between devices: 267 us -> 334 us
  local copies, waits for them, and re-layouts: 202 us -> 214 us
    all_gather x2 -> x1, waiting for transfers between devices: 33.2 us -> 100 us  [per_device(): lax.all_gather(jnp.concatenate([k_proj, hyena_out], axis=1), 'seq', axis=...]
    unnamed x17 -> x22, local copies, waits for them, and re-layouts: 49.5 us -> 61.6 us
  transfers between devices with their start and end apart: 5 -> 4, of which waited for: 2 -> 2; matrix products, arithmetic and copies ran while one was open for 40% -> 5% of each run, Pallas kernels for 0% -> 0%
where the time goes in v1:
time: 725 us; the launch traced here: 717 us
  waiting for transfers between devices  334 us (46%)
  local copies, waits for them, and re-layouts  214 us (30%)
  matrix products  106 us (15%)
  other arithmetic  36.6 us (5%)
  between operations  14.4 us (2%)
  starting transfers between devices  7.74 us (1%)
    reduce_scatter x1, waiting for transfers between devices, per_device(): lax.psum_scatter(lax.dot_general(out_weight, attended, (((0,), (1,)), (()...  234 us
    all_gather x1, waiting for transfers between devices, per_device(): lax.all_gather(jnp.concatenate([k_proj, hyena_out], axis=1), 'seq', axis=...  100 us
    conv_general_dilated x7, local copies, waits for them, and re-layouts, causal_depthwise(): lax.conv_general_dilated(window[None], kernel, (1,), 'VALID', feature_gro...  90.1 us
    unnamed x22, local copies, waits for them, and re-layouts  61.6 us
    conv_general_dilated x2, matrix products, causal_depthwise(): lax.conv_general_dilated(window[None], kernel, (1,), 'VALID', feature_gro...  59.9 us
    dot_general x1, matrix products, per_device(): lax.dot_general(out_weight, attended, (((0,), (1,)), ((), ())), preferred...  26 us
    rev x2, local copies, waits for them, and re-layouts, causal_depthwise(): kernel = taps[::-1][:, None, :]  22 us
  transfers between devices with their start and end apart: 4, of which 2 were waited for; matrix products, arithmetic and copies ran while one was open for 5% of the time, Pallas kernels for 0%

profile of v1, /device:TPU:0, one launch (start us, length us, event | category | flops | bytes accessed | tf_op | source)
XLA Modules:
  0.0 716.8 jit_solution(5799570980599447031)
XLA Ops:
  10.5 16.9 %rev.6 = f32[3,6144]{1,0:T(4,128)S(1)} reverse(f32[3,6144]{1,0:T(4,128)} %bitcast.76), dimensions={0} | reverse | bytes 147456 | tf_op jit(solution)/shard_map/rev | solution.py:19
  27.4 7.8 %pad_maximum_fusion = bf16[514,3,2048]{2,0,1:T(8,128)(2,1)} fusion(bf16[512,3,2048]{2,0,1:T(8,128)(2,1)} %param.10, bf16[2,3,2048]{2,0,1:T(2,128)(2,1)S(1)} %collective-permute-done), kind=kLoop, calls=%fused_computation.39 | loop fusion | flops 12632064 | bytes 12632064 | tf_op jit(solution)/shard_map/concatenate | solution.py:40
  35.3 9.7 %copy.13 = bf16[514,3,2048]{0,2,1:T(8,128)(2,1)} copy(bf16[514,3,2048]{2,0,1:T(8,128)(2,1)} %pad_maximum_fusion) | data formatting | bytes 12632064 | tf_op jit(solution)/shard_map/concatenate | solution.py:40
  45.0 7.0 pad
  52.0 20.5 %reshape.76 = bf16[1,8,65,6144]{2,1,3,0:T(8,128)(2,1)} reshape(bf16[1,520,6144]{1,2,0:T(8,128)(2,1)} %pad) | data formatting | bytes 12779520 | tf_op jit(solution)/shard_map/conv_general_dilated | solution.py:20
  72.5 16.8 %copy.16 = bf16[1,8,65,6144]{3,1,2,0:T(8,128)(2,1)} copy(bf16[1,8,65,6144]{2,1,3,0:T(8,128)(2,1)} %reshape.76) | data formatting | bytes 12779520 | tf_op jit(solution)/shard_map/conv_general_dilated | solution.py:20
  90.3 11.5 %fusion.30 = f32[8,65,6144]{2,0,1:T(8,128)} fusion(f32[3,1,6144]{2,1,0:T(1,128)S(1)} %broadcast_in_dim.40, bf16[1,7,2,6144]{3,1,2,0:T(8,128)(2,1)S(1)} %slice.26, bf16[1,8,65,6144]{3,1,2,0:T(8,128)(2,1)} %copy.16, pred[8,65]{0,1:T(8,128)(4,1)S(1)} %copy-done.6), kind=kOutput, calls=%fused_computation.35 | convolution fusion | flops 137969664 | bytes 19415560 | tf_op jit(solution)/shard_map/conv_general_dilated | solution.py:20
  101.8 17.2 %copy.17 = f32[8,65,6144]{2,1,0:T(8,128)} copy(f32[8,65,6144]{2,0,1:T(8,128)} %fusion.30) | data formatting | bytes 25559040 | tf_op jit(solution)/shard_map/conv_general_dilated | solution.py:20
  119.0 11.3 %reshape.72 = f32[1,520,6144]{2,1,0:T(8,128)} reshape(f32[8,65,6144]{2,1,0:T(8,128)} %copy.17) | data formatting | bytes 25559040 | tf_op jit(solution)/shard_map/conv_general_dilated | solution.py:20
  130.2 10.6 %slice.27 = f32[1,512,6144]{2,1,0:T(8,128)} slice(f32[1,520,6144]{2,1,0:T(8,128)} %reshape.72), slice={[0:1], [0:512], [0:6144]} | slice | bytes 25165824 | tf_op jit(solution)/shard_map/conv_general_dilated | solution.py:20
  140.8 12.8 %copy.18 = f32[1,512,6144]{1,2,0:T(8,128)} copy(f32[1,512,6144]{2,1,0:T(8,128)} %slice.27) | data formatting | bytes 25165824 | tf_op jit(solution)/shard_map/conv_general_dilated | solution.py:20
  153.6 7.7 %fusion.44 = (f32[512,1,2048]{0,2,1:T(8,128)}, bf16[512,1,2048]{0,2,1:T(8,128)(2,1)S(1)}) fusion(f32[512,3,2048]{0,2,1:T(8,128)} %bitcast.68), kind=kLoop, calls=%fused_computation.54 | loop fusion | flops 2097152 | bytes 18874368 | tf_op jit(solution)/shard_map/slice | solution.py:49
  162.3 5.3 collective-permute-start.1
  167.6 5.2 rev.7
  172.8 5.5 copy.34
  178.3 4.0 maximum_bitcast_fusion
  182.3 11.5 %copy.21 = bf16[1,639,2048]{2,0,1:T(2,128)(2,1)} copy(bf16[1,639,2048]{1,2,0:T(8,128)(2,1)} %maximum_bitcast_fusion) | data formatting | bytes 5234688 | tf_op jit(solution)/shard_map/broadcast_in_dim | solution.py:21
  193.8 48.5 %fusion.39 = f32[1,512,2048]{2,0,1:T(1,128)S(1)} fusion(bf16[1,639,2048]{2,0,1:T(2,128)(2,1)} %copy.21, f32[128,1,2048]{2,0,1:T(8,128)S(1)} %bitcast.75), kind=kOutput, calls=%fused_computation.48 | convolution fusion | flops 1610612736 | bytes 7860224 | tf_op jit(solution)/shard_map/conv_general_dilated | solution.py:20
  254.6 100.4 %all-gather.2.cloned.1.call-done = bf16[2048,4096]{1,0:T(8,128)(2,1)} async-done(((bf16[512,4096]{1,0:T(8,128)(2,1)}), bf16[2048,4096]{1,0:T(8,128)(2,1)}) %all-gather.2.cloned.1.call-update) | async-done | bytes 16777232 | tf_op jit(solution)/shard_map/all_gather | solution.py:64
  354.9 11.8 %slice_bitcast_fusion = (bf16[256,8,16,128]{3,1,2,0:T(8,128)(2,1)}, bf16[256,8,16,128]{3,1,2,0:T(8,128)(2,1)}) fusion(bf16[2048,4096]{1,0:T(8,128)(2,1)} %all-gather.2.cloned.1.call-done), kind=kLoop, calls=%fused_computation.30 | loop fusion | bytes 33554432
  366.8 9.8 %copy.35 = bf16[256,8,16,128]{3,2,1,0:T(8,128)(2,1)} copy(bf16[256,8,16,128]{3,1,2,0:T(8,128)(2,1)} %get-tuple-element.216) | data formatting | bytes 16777216
  376.5 8.8 %copy.24 = bf16[4,512,16,128]{3,1,2,0:T(8,128)(2,1)} copy(bf16[4,512,16,128]{3,2,1,0:T(8,128)(2,1)} %bitcast.69) | data formatting | bytes 16777216
  385.3 9.8 %copy.36 = bf16[256,8,16,128]{3,2,1,0:T(8,128)(2,1)} copy(bf16[256,8,16,128]{3,1,2,0:T(8,128)(2,1)} %get-tuple-element.215) | data formatting | bytes 16777216
  395.1 8.8 %copy.26 = bf16[4,512,16,128]{3,1,2,0:T(8,128)(2,1)} copy(bf16[4,512,16,128]{3,2,1,0:T(8,128)(2,1)} %bitcast.70) | data formatting | bytes 16777216
  406.3 35.1 %while.15 = (s32[]{:T(128)}, f32[16,512,128]{2,1,0:T(8,128)}, f32[16,512]{1,0:T(8,128)S(1)}, f32[16,512]{1,0:T(8,128)S(1)}, s32[4]{0:T(128)S(1)}, /*index=5*/s32...) while((s32[]{:T(128)}, f32[16,512,128]{2,1,0:T(8,128)}, ...), condition=%wide.region_5.6_spmd.clone, body=%wide.region_0.5_spmd.clone.sunk | while | flops 2195997696 | bytes 66598184 | solution.py:104
  407.7 30.0 %conditional.3 = ((f32[16,512,128]{2,1,0:T(8,128)}, f32[16,512]{1,0:T(8,128)S(1)}, f32[16,512]{1,0:T(8,128)S(1)})) conditional(s32[]{:T(128)} %convert_element_type.60, (f32[16,512,128]{2,1,0:T(8,128)}, f32[16,512]{1,0:T(8,128)S(1)}, f32[16,512]{1,0:T(8,128)S(1)}) %tuple.47, (s32[]{:T(128)}, s32[]{:T(128)}, bf16[4,512,16,128]{3,1,2,0:T(8,128)(2,1)}, ...), branch_computations={%region_1.1_spmd, %region_2.4_spmd} | conditional | flops 2195997696 | bytes 66595880 | solution.py:102
  408.0 8.8 %fusion.4 = (f32[16,512]{1,0:T(8,128)S(1)}, f32[16,512,512]{2,1,0:T(8,128)}) fusion(pred[512,512]{0,1:T(8,128)(4,1)S(1)} %broadcast_compare_fusion, bf16[512,16,128]{2,0,1:T(8,128)(2,1)S(1)} %get-tuple-element.117, bf16[4,512,16,128]{3,1,2,0:T(8,128)(2,1)} %get-tuple-element.115, s32[]{:T(128)} %get-tuple-element.116), kind=kOutput, calls=%fused_computation.5 | convolution fusion | flops 1086316544 | bytes 21266944 | tf_op jit(solution)/shard_map/while/body/eval_jaxpr/cond/branch_1_fun/qhd,khd->hqk/dot_general | solution.py:81
  416.8 9.1 %fusion.2 = f32[16,512]{1,0:T(8,128)S(1)} fusion(f32[16,512,512]{2,1,0:T(8,128)} %get-tuple-element.212, f32[16,512]{1,0:T(8,128)S(1)} %max.4, pred[512,512]{0,1:T(8,128)(4,1)S(1)} %broadcast_compare_fusion), kind=kLoop, calls=%fused_computation.3 | loop fusion | flops 16769024 | bytes 17104896 | tf_op jit(solution)/shard_map/while/body/eval_jaxpr/cond/branch_1_fun/reduce_sum | solution.py:90
  425.9 11.7 %multiply_add_fusion = f32[16,512,128]{2,1,0:T(8,128)} fusion(f32[16,512,128]{2,1,0:T(8,128)} %get-tuple-element.111, f32[16,512]{1,0:T(8,128)S(1)} %get-tuple-element.210, bf16[4,512,16,128]{3,1,2,0:T(8,128)(2,1)} %get-tuple-element.118, s32[]{:T(128)} %get-tuple-element.116, f32[16,512,512]{2,1,0:T(8,128)} %get-tuple-element.212, f32[16,512]{1,0:T(8,128)S(1)} %max.4, ...), kind=kOutput, calls=%fused_computation.11 | convolution fusion | flops 1092616192 | bytes 27591168 | tf_op jit(solution)/shard_map/while/body/eval_jaxpr/cond/branch_1_fun/hqk,khd->hqd/dot_general | solution.py:91
  441.5 5.4 copy.27
  449.7 26.0 %fusion.25 = bf16[8192,512]{0,1:T(8,128)(2,1)} fusion(bf16[512,2048]{0,1:T(8,128)(2,1)S(1)} %bitcast.74, bf16[2048,8192]{1,0:T(8,128)(2,1)} %param.15), kind=kOutput, calls=%fused_computation.29 | convolution fusion | flops 17184063488 | bytes 44040192 | tf_op jit(solution)/shard_map/dot_general | solution.py:115
  475.7 234.0 %reduce-scatter.2.cloned.1.call-done = bf16[2048,512]{0,1:T(8,128)(2,1)} async-done(((bf16[8192,512]{0,1:T(8,128)(2,1)}), bf16[2048,512]{0,1:T(8,128)(2,1)}) %reduce-scatter.2.cloned.1.call-update) | async-done | bytes 2097168 | tf_op jit(solution)/shard_map/reduce_scatter | solution.py:114
  (50 shorter events, 25.5 us)
Async XLA Ops:
  7.2 347.8 %all-gather.2.cloned.1.call-start = ((), (), s32[]{:S(2)}) async-start(), calls=%async_computation.1 | async-start | bytes 20971520 | tf_op jit(solution)/shard_map/all_gather | solution.py:64
  8.1 19.3 %collective-permute-start = (bf16[2,3,2048]{2,0,1:T(2,128)(2,1)S(1)}, bf16[2,3,2048]{2,0,1:T(2,128)(2,1)S(1)}, u32[]{:S(2)}, u32[]{:S(2)}) collective-permute-start(bf16[2,3,2048]{2,0,1:T(2,128)(2,1)S(1)} %slice.18), channel_id=1, source_target_pairs={{0,8},{8,16},{16,24},{1,9},{9,17},{17,25},{2,10},{10,18},{18,26},{... | collective-permute-start | bytes 73736 | tf_op jit(solution)/shard_map/ppermute | solution.py:13
  72.5 17.8 %copy-start.6 = (pred[8,65]{0,1:T(8,128)(4,1)S(1)}, pred[8,65]{0,1:T(8,128)(4,1)}, u32[]{:S(2)}) copy-start(pred[8,65]{0,1:T(8,128)(4,1)} %constant.55) | copy-start | bytes 1564
  153.6 14.0 %copy-start.4 = (f32[128,2048]{1,0:T(8,128)S(1)}, f32[128,2048]{1,0:T(8,128)}, u32[]{:S(2)}) copy-start(f32[128,2048]{1,0:T(8,128)} %param.12) | copy-start | bytes 3145732
  162.3 15.9 %collective-permute-start.1 = (bf16[127,2048]{0,1:T(8,128)(2,1)}, bf16[127,2048]{0,1:T(8,128)(2,1)}, u32[]{:S(2)}, u32[]{:S(2)}) collective-permute-start(bf16[127,2048]{0,1:T(8,128)(2,1)} %slice_bitcast_fusion.2), channel_id=1, source_target_pairs={{0,8},{8,16},{16,24},{1,9},{9,17},{17,25},{2,10},{10,18},{18,26},{... | collective-permute-start | bytes 1560584 | tf_op jit(solution)/shard_map/ppermute | solution.py:13
  178.3 15.6 %copy-start.5 = (f32[128,2048]{1,0:T(8,128)S(1)}, f32[128,2048]{1,0:T(8,128)}, u32[]{:S(2)}) copy-start(f32[128,2048]{1,0:T(8,128)} %rev.7) | copy-start | bytes 3145732
  193.8 48.5 %copy-start = (f32[512,1,2048]{2,0,1:T(8,128)S(1)}, f32[512,1,2048]{2,0,1:T(8,128)}, u32[]{:S(2)}) copy-start(f32[512,1,2048]{2,0,1:T(8,128)} %copy.34) | copy-start | bytes 12582916
  242.3 3.7 copy-start.3
  244.8 1.3 copy-start.1
  246.1 2.5 copy-start.2
  248.5 461.2 %reduce-scatter.2.cloned.1.call-start = ((), (), s32[]{:S(2)}) async-start(), calls=%async_computation.2 | async-start | bytes 10485760 | tf_op jit(solution)/shard_map/reduce_scatter | solution.py:114
Sparse Core Ops, SparseCore 0:
  248.7 106.2 all-gather.1
  475.8 233.8 reduce-scatter.1
